TPU v7x, 512 devices: a whole 4x4x16 slice. The times are simulated.
512 devices in a mesh: rows: 32 (over y, x, core), cols: 16 (over z).
Axes of the slice: x: 4, y: 4, z: 16, core: 2. Of those that a mesh axis runs over, the one named last changes fastest.
Arguments:
- encoded: bfloat16 [1024, 512, 384], P('rows', 'cols'), may hold values from -6 to 6
- conv_weight: bfloat16 [3, 3, 384, 384], replicated, may hold values from -0.109375 to 0.109375
- film_table: bfloat16 [360, 2, 384], replicated, may hold values from -3 to 3
- lead: int32 [1], replicated, may hold values from 0 to 359
Outputs:
- updated: bfloat16 [1024, 512, 384], P('rows', 'cols')
All inputs are finite; a program needn't handle non-finite values.
Results may differ from a plain program's by a relative error of at most 0.006.
Values may be sent and summed in bfloat16 or wider, within the bound.
A program may use at most 64 MiB of HBM per device.

v0:
```python
import jax
import jax.numpy as jnp
from jax import lax
from jax.sharding import PartitionSpec as P

DILATION_RATE = 128


def shifted(block, axis, distance):
    devices = range(lax.axis_size(axis))
    route = [(i - distance, i) for i in devices if i - distance in devices]
    return lax.ppermute(block, axis, route)


def tap_product(group, filter_kernel):
    count = group.shape[0]
    grid_height, grid_width, chans = (group.shape[1], group.shape[2], group.shape[3])
    flat = jnp.concatenate(
        [group[k].reshape(grid_height * grid_width, chans) for k in range(count)], axis=1
    )
    return jnp.dot(
        flat,
        filter_kernel.reshape(count * chans, filter_kernel.shape[-1]),
        preferred_element_type=jnp.float32,
    )


def local(encoded, conv_weight, film_table, lead):
    grid_height, grid_width, chans = encoded.shape
    active = jnp.maximum(encoded, jnp.zeros((), jnp.bfloat16))
    row_step = DILATION_RATE // grid_height
    column_step = DILATION_RATE // grid_width
    row_reach = row_step < lax.axis_size("rows")
    column_extent = column_step < lax.axis_size("cols")
    lower = shifted(active, "rows", row_step)
    upper = shifted(active, "rows", -row_step)
    middle = jnp.stack([lower, active, upper])
    total = tap_product(middle, conv_weight[:, 1])
    left = shifted(middle, "cols", column_step)
    right = shifted(middle, "cols", -column_step)
    total = total + tap_product(left, conv_weight[:, 0])
    total = total + tap_product(right, conv_weight[:, 2])
    leads = film_table.shape[0]
    onehot = (jnp.arange(leads, dtype=jnp.int32) == lead[0]).astype(jnp.bfloat16)[None]
    selected_taps = jnp.dot(
        onehot, film_table.reshape(leads, 2 * chans), preferred_element_type=jnp.float32
    )
    gamma = selected_taps[0, :chans]
    beta = selected_taps[0, chans:]
    conv = total.reshape(grid_height, grid_width, chans)
    updated = encoded.astype(jnp.float32) + conv * (1.0 + gamma) + beta
    return updated.astype(jnp.bfloat16)


def solution(mesh):
    placed = (P("rows", "cols", None), P(), P(), P())
    return jax.shard_map(
        local, mesh=mesh, in_specs=placed, out_specs=P("rows", "cols", None), check_vma=False
    )
```

profile of v0, /device:TPU:24, one launch (start us, length us, event | category | flops | bytes accessed | tf_op | source)
XLA Modules:
  0.0 264.3 jit_solution(16653005359593306372)
XLA Ops:
  0.0 1.3 fusion.24
  1.3 5.1 %collective-permute-start.1 = (bf16[32,32,384]{2,1,0:T(8,128)(2,1)S(1)}, bf16[32,32,384]{2,1,0:T(8,128)(2,1)S(1)}, u32[]{:S(2)}, u32[]{:S(2)}) collective-permute-start(bf16[32,32,384]{2,1,0:T(8,128)(2,1)S(1)} %get-tuple-element.17), channel_id=1, source_target_pairs={{64,0},{80,16},{96,32},{112,48},{128,64},{144,80},{160,96},{176,11... | collective-permute-start | bytes 2359304 | tf_op jit(solution)/shard_map/ppermute | solution.py:12
  6.4 2.3 collective-permute-start
  8.7 15.6 %collective-permute-done.1 = bf16[32,32,384]{2,1,0:T(8,128)(2,1)S(1)} collective-permute-done((bf16[32,32,384]{2,1,0:T(8,128)(2,1)S(1)}, bf16[32,32,384]{2,1,0:T(8,128)(2,1)S(1)}, u32[]{:S(2)}, u32[]{:S(2)}) %collective-permute-start.1) | collective-permute-done | bytes 786464 | tf_op jit(solution)/shard_map/ppermute | solution.py:12
  24.3 16.7 %collective-permute-done = bf16[32,32,384]{2,1,0:T(8,128)(2,1)S(1)} collective-permute-done((bf16[32,32,384]{2,1,0:T(8,128)(2,1)S(1)}, bf16[32,32,384]{2,1,0:T(8,128)(2,1)S(1)}, u32[]{:S(2)}, u32[]{:S(2)}) %collective-permute-start) | collective-permute-done | bytes 786464 | tf_op jit(solution)/shard_map/ppermute | solution.py:12
  41.0 0.0 copy-start.2
  41.0 0.0 copy-start.1
  41.0 0.3 pad_maximum_fusion
  41.3 9.4 %collective-permute-start.2 = (bf16[3,32,32,384]{3,2,1,0:T(8,128)(2,1)S(1)}, bf16[3,32,32,384]{3,2,1,0:T(8,128)(2,1)S(1)}, u32[]{:S(2)}, u32[]{:S(2)}) collective-permute-start(bf16[3,32,32,384]{3,2,1,0:T(8,128)(2,1)S(1)} %pad_maximum_fusion), channel_id=1, source_target_pairs={{0,4},{1,5},{2,6},{3,7},{4,8},{5,9},{6,10},{7,11},{8,12},{9,13},{1... | collective-permute-start | bytes 7077896 | tf_op jit(solution)/shard_map/ppermute | solution.py:12
  50.7 1.3 collective-permute-start.3
  52.7 0.0 copy-done.2
  52.7 0.1 copy.5
  52.8 0.2 fusion.28
  53.0 0.0 copy-done.1
  53.0 0.3 fusion.25
  53.3 1.4 fusion
  54.7 45.6 %collective-permute-done.2 = bf16[3,32,32,384]{3,2,1,0:T(8,128)(2,1)S(1)} collective-permute-done((bf16[3,32,32,384]{3,2,1,0:T(8,128)(2,1)S(1)}, bf16[3,32,32,384]{3,2,1,0:T(8,128)(2,1)S(1)}, u32[]{:S(2)}, u32[]{:S(2)}) %collective-permute-start.2) | collective-permute-done | bytes 2359328 | tf_op jit(solution)/shard_map/ppermute | solution.py:12
  100.3 0.2 fusion.27
  100.5 1.4 fusion.6
  102.0 159.4 %collective-permute-done.3 = bf16[3,32,32,384]{3,2,1,0:T(8,128)(2,1)S(1)} collective-permute-done((bf16[3,32,32,384]{3,2,1,0:T(8,128)(2,1)S(1)}, bf16[3,32,32,384]{3,2,1,0:T(8,128)(2,1)S(1)}, u32[]{:S(2)}, u32[]{:S(2)}) %collective-permute-start.3) | collective-permute-done | bytes 2359328 | tf_op jit(solution)/shard_map/ppermute | solution.py:12
  261.4 0.2 fusion.26
  261.6 0.0 copy-start
  261.7 1.5 add_add_fusion
  263.1 0.0 copy-done
  263.2 1.2 add_convert_fusion
  (3 shorter events, 0.1 us)
Async XLA Ops:
  1.3 23.0 %collective-permute-start.1 = (bf16[32,32,384]{2,1,0:T(8,128)(2,1)S(1)}, bf16[32,32,384]{2,1,0:T(8,128)(2,1)S(1)}, u32[]{:S(2)}, u32[]{:S(2)}) collective-permute-start(bf16[32,32,384]{2,1,0:T(8,128)(2,1)S(1)} %get-tuple-element.17), channel_id=1, source_target_pairs={{64,0},{80,16},{96,32},{112,48},{128,64},{144,80},{160,96},{176,11... | collective-permute-start | bytes 2359304 | tf_op jit(solution)/shard_map/ppermute | solution.py:12
  6.4 34.6 %collective-permute-start = (bf16[32,32,384]{2,1,0:T(8,128)(2,1)S(1)}, bf16[32,32,384]{2,1,0:T(8,128)(2,1)S(1)}, u32[]{:S(2)}, u32[]{:S(2)}) collective-permute-start(bf16[32,32,384]{2,1,0:T(8,128)(2,1)S(1)} %get-tuple-element.17), channel_id=1, source_target_pairs={{0,64},{16,80},{32,96},{48,112},{64,128},{80,144},{96,160},{112,17... | collective-permute-start | bytes 2359304 | tf_op jit(solution)/shard_map/ppermute | solution.py:12
  41.0 11.7 %copy-start.2 = (bf16[360,2,384]{2,1,0:T(2,128)(2,1)S(1)}, bf16[360,2,384]{2,1,0:T(2,128)(2,1)}, u32[]{:S(2)}) copy-start(bf16[360,2,384]{2,1,0:T(2,128)(2,1)} %param.6) | copy-start | bytes 1658884
  41.0 12.0 %copy-start.1 = (bf16[3,3,384,384]{3,2,1,0:T(8,128)(2,1)S(1)}, bf16[3,3,384,384]{3,2,1,0:T(8,128)(2,1)}, u32[]{:S(2)}) copy-start(bf16[3,3,384,384]{3,2,1,0:T(8,128)(2,1)} %param.5) | copy-start | bytes 7962628
  41.3 59.0 %collective-permute-start.2 = (bf16[3,32,32,384]{3,2,1,0:T(8,128)(2,1)S(1)}, bf16[3,32,32,384]{3,2,1,0:T(8,128)(2,1)S(1)}, u32[]{:S(2)}, u32[]{:S(2)}) collective-permute-start(bf16[3,32,32,384]{3,2,1,0:T(8,128)(2,1)S(1)} %pad_maximum_fusion), channel_id=1, source_target_pairs={{0,4},{1,5},{2,6},{3,7},{4,8},{5,9},{6,10},{7,11},{8,12},{9,13},{1... | collective-permute-start | bytes 7077896 | tf_op jit(solution)/shard_map/ppermute | solution.py:12
  50.7 210.7 %collective-permute-start.3 = (bf16[3,32,32,384]{3,2,1,0:T(8,128)(2,1)S(1)}, bf16[3,32,32,384]{3,2,1,0:T(8,128)(2,1)S(1)}, u32[]{:S(2)}, u32[]{:S(2)}) collective-permute-start(bf16[3,32,32,384]{3,2,1,0:T(8,128)(2,1)S(1)} %pad_maximum_fusion), channel_id=1, source_target_pairs={{4,0},{5,1},{6,2},{7,3},{8,4},{9,5},{10,6},{11,7},{12,8},{13,9},{1... | collective-permute-start | bytes 7077896 | tf_op jit(solution)/shard_map/ppermute | solution.py:12
  261.6 1.5 copy-start
where the time goes:
time: 265 us; the launch traced here: 264 us
  waiting for transfers between devices  237 us (89%)
  starting transfers between devices  18.1 us (7%)
  matrix products  4.53 us (2%)
  other arithmetic  2.79 us (1%)
    ppermute x4, waiting for transfers between devices, shifted(): return lax.ppermute(block, axis, route)  237 us
    ppermute x4, starting transfers between devices, shifted(): return lax.ppermute(block, axis, route)  18.1 us
  transfers between devices with their start and end apart: 4, of which 4 were waited for; matrix products, arithmetic and copies ran while one was open for 1% of the time, Pallas kernels for 0%

commit v1 on v0

v1 whole, which is shorter than its diff:
```python
import functools

import jax
import jax.numpy as jnp
from jax import lax
from jax.experimental import pallas as pl
from jax.experimental.pallas import tpu as pltpu
from jax.sharding import PartitionSpec as P

DILATION_RATE = 128
CHUNKS = 8
AHEAD = 2
CELLS = 16
MESH = pl.DeviceIdType.MESH


def kernel(dims, lead, enc_hbm, w_hbm, film_hbm, out_hbm, enc, w, film, mid, left, right, done,
           load_sem, own_sem, in_send, in_recv, col_send, col_recv, out_send, out_recv):
    n_rows, n_cols, row_step, col_step = dims
    per = enc.shape[0] // n_rows
    take = per // CHUNKS
    row, col = lax.axis_index("rows"), lax.axis_index("cols")
    me, lane = row // row_step, row % row_step
    has_left, has_right = col >= col_step, col < (n_cols - 1) * col_step

    def peer(step):
        other = lax.rem(me + step, n_rows)
        return other, (other * row_step + lane, col)

    def source(step):
        return lax.rem(me + n_rows - step, n_rows)

    loads = [
        pltpu.make_async_copy(enc_hbm, enc, load_sem.at[0]),
        pltpu.make_async_copy(w_hbm, w, load_sem.at[1]),
        pltpu.make_async_copy(film_hbm, film, load_sem.at[2]),
    ]
    for load in loads:
        load.start()

    barrier = pltpu.get_barrier_semaphore()

    def greet(step, carry):
        pl.semaphore_signal(barrier, inc=1, device_id=peer(step)[1], device_id_type=MESH)
        return carry

    @pl.when(has_left)
    def _():
        pl.semaphore_signal(barrier, inc=1, device_id=(row, col - col_step), device_id_type=MESH)

    @pl.when(has_right)
    def _():
        pl.semaphore_signal(barrier, inc=1, device_id=(row, col + col_step), device_id_type=MESH)

    lax.fori_loop(1, n_rows, greet, 0)

    for buffer in (mid, left, right):
        zero = jnp.zeros(buffer.shape[:1] + buffer.shape[2:], buffer.dtype)
        buffer[:, 0] = zero
        buffer[:, n_rows + 1] = zero

    @pl.when(jnp.logical_not(has_left))
    def _():
        left[...] = jnp.zeros_like(left)

    @pl.when(jnp.logical_not(has_right))
    def _():
        right[...] = jnp.zeros_like(right)

    loads[0].wait()
    greeted = n_rows - 1 + has_left.astype(jnp.int32) + has_right.astype(jnp.int32)
    pl.semaphore_wait(barrier, greeted)

    def own_copy(part):
        return pltpu.make_async_copy(
            enc.at[pl.ds(me * per + part * take, take)], mid.at[part, me + 1], own_sem.at[part])

    def in_copy(part, step):
        other, device = peer(step)
        return pltpu.make_async_remote_copy(
            src_ref=enc.at[pl.ds(other * per + part * take, take)],
            dst_ref=mid.at[part, me + 1],
            send_sem=in_send.at[part, step],
            recv_sem=in_recv.at[part, step],
            device_id=device, device_id_type=MESH)

    def in_arrival(part, step):
        return pltpu.make_async_remote_copy(
            src_ref=enc.at[pl.ds(0, take)],
            dst_ref=mid.at[part, source(step) + 1],
            send_sem=in_send.at[part, step],
            recv_sem=in_recv.at[part, step],
            device_id=peer(step)[1], device_id_type=MESH)

    def col_copy(part, way):
        buffer, shift = ((left, col_step), (right, -col_step))[way]
        return pltpu.make_async_remote_copy(
            src_ref=mid.at[part, pl.ds(1, n_rows)],
            dst_ref=buffer.at[part, pl.ds(1, n_rows)],
            send_sem=col_send.at[part, way],
            recv_sem=col_recv.at[part, way],
            device_id=(row, col + shift), device_id_type=MESH)

    def out_copy(part, step):
        other, device = peer(step)
        return pltpu.make_async_remote_copy(
            src_ref=done.at[part, other],
            dst_ref=out_hbm.at[pl.ds(me * per + part * take, take)],
            send_sem=out_send.at[part, step],
            recv_sem=out_recv.at[part, step],
            device_id=device, device_id_type=MESH)

    def out_arrival(part, step):
        return pltpu.make_async_remote_copy(
            src_ref=done.at[part, 0],
            dst_ref=out_hbm.at[pl.ds(source(step) * per + part * take, take)],
            send_sem=out_send.at[part, step],
            recv_sem=out_recv.at[part, step],
            device_id=peer(step)[1], device_id_type=MESH)

    def out_own(part):
        return pltpu.make_async_copy(
            done.at[part, me], out_hbm.at[pl.ds(me * per + part * take, take)], own_sem.at[CHUNKS + part])

    def each(first, last, act):
        def body(step, carry):
            act(step)
            return carry
        lax.fori_loop(first, last, body, 0)

    def spread(part):
        own_copy(part).start()
        each(1, n_rows, lambda step: in_copy(part, step).start())

    def send_columns(part):
        @pl.when(has_right)
        def _():
            col_copy(part, 0).start()

        @pl.when(has_left)
        def _():
            col_copy(part, 1).start()

    def columns_sent(part):
        @pl.when(has_right)
        def _():
            col_copy(part, 0).wait_send()

        @pl.when(has_left)
        def _():
            col_copy(part, 1).wait_send()

    def columns_arrived(part):
        @pl.when(has_left)
        def _():
            col_copy(part, 0).wait_recv()

        @pl.when(has_right)
        def _():
            col_copy(part, 1).wait_recv()

    chans = enc.shape[-1]
    cells = n_rows * take * CELLS

    def compute(part):
        picked = film[lead[0]].astype(jnp.float32)
        gamma, beta = picked[0:1], picked[1:2]
        total = jnp.zeros((cells, chans), jnp.float32)
        for kx, buffer in enumerate((left, mid, right)):
            for ky in range(3):
                block = jnp.maximum(buffer[part, pl.ds(ky, n_rows)], 0).reshape(cells, chans)
                total += jnp.dot(block, w[ky, kx], preferred_element_type=jnp.float32)
        here = mid[part, pl.ds(1, n_rows)].reshape(cells, chans).astype(jnp.float32)
        updated = here + total * (1.0 + gamma) + beta
        done[part] = updated.astype(jnp.bfloat16).reshape(done.shape[1:])

    each(0, 2, spread)

    def stage(part, carry):
        @pl.when(part < CHUNKS)
        def _():
            own_copy(part).wait()
            each(1, n_rows, lambda step: in_arrival(part, step).wait_recv())

            @pl.when(part >= AHEAD)
            def _():
                columns_sent(part - AHEAD)

            send_columns(part)

            @pl.when(part + 2 < CHUNKS)
            def _():
                spread(part + 2)

        @pl.when(part == 0)
        def _():
            loads[1].wait()
            loads[2].wait()

        @pl.when(part >= AHEAD)
        def _():
            ready = part - AHEAD
            columns_arrived(ready)
            compute(ready)
            out_own(ready).start()
            each(1, n_rows, lambda step: out_copy(ready, step).start())

        return carry

    lax.fori_loop(0, CHUNKS + AHEAD, stage, 0)

    def finish(part):
        @pl.when(part >= CHUNKS - AHEAD)
        def _():
            columns_sent(part)

        out_own(part).wait()

        def one(step):
            in_copy(part, step).wait_send()
            out_copy(part, step).wait_send()
            out_arrival(part, step).wait_recv()

        each(1, n_rows, one)

    each(0, CHUNKS, finish)


def local(encoded, conv_weight, film_table, lead):
    height, width, chans = encoded.shape
    row_step, col_step = DILATION_RATE // height, DILATION_RATE // width
    n_rows = lax.axis_size("rows") // row_step
    n_cols = lax.axis_size("cols") // col_step
    units = height * width // CELLS
    take = units // n_rows // CHUNKS
    padded = (CHUNKS, n_rows + 2, take, CELLS, chans)
    hbm = pl.BlockSpec(memory_space=pltpu.HBM)
    dma = pltpu.SemaphoreType.DMA
    updated = pl.pallas_call(
        functools.partial(kernel, (n_rows, n_cols, row_step, col_step)),
        out_shape=jax.ShapeDtypeStruct((units, CELLS, chans), jnp.bfloat16),
        in_specs=[pl.BlockSpec(memory_space=pltpu.SMEM)] + [hbm] * 3,
        out_specs=pl.BlockSpec(memory_space=pl.ANY),
        scratch_shapes=[
            pltpu.VMEM((units, CELLS, chans), jnp.bfloat16),
            pltpu.VMEM(conv_weight.shape, jnp.bfloat16),
            pltpu.VMEM(film_table.shape, jnp.bfloat16),
            pltpu.VMEM(padded, jnp.bfloat16),
            pltpu.VMEM(padded, jnp.bfloat16),
            pltpu.VMEM(padded, jnp.bfloat16),
            pltpu.VMEM((CHUNKS, n_rows, take, CELLS, chans), jnp.bfloat16),
            dma((3,)),
            dma((2 * CHUNKS,)),
            dma((CHUNKS, n_rows)),
            dma((CHUNKS, n_rows)),
            dma((CHUNKS, 2)),
            dma((CHUNKS, 2)),
            dma((CHUNKS, n_rows)),
            dma((CHUNKS, n_rows)),
        ],
        compiler_params=pltpu.CompilerParams(
            collective_id=0, has_side_effects=True, vmem_limit_bytes=40 * 1024 * 1024),
        cost_estimate=pl.CostEstimate(
            flops=2 * 9 * height * width * chans * chans, bytes_accessed=5_000_000, transcendentals=0),
        name="dilated_block",
    )(lead, encoded.reshape(units, CELLS, chans), conv_weight, film_table)
    return updated.reshape(encoded.shape)


def solution(mesh):
    placed = (P("rows", "cols", None), P(), P(), P())
    return jax.shard_map(
        local, mesh=mesh, in_specs=placed, out_specs=P("rows", "cols", None), check_vma=False
    )
```

time: 265 us -> 106 us (0.40)
  the two profiles are of different devices: /device:TPU:24 before, /device:TPU:128 now
where the time goes in v1:
time: 106 us
  Pallas kernels  100 us (94%)
  local copies, waits for them, and re-layouts  4.81 us (5%)
    pallas_call x1, Pallas kernels, local(): pl.pallas_call(functools.partial(kernel, (n_rows, n_cols, row_step, col_s...  100 us
    unnamed x7, local copies, waits for them, and re-layouts  4.81 us

profile of v1, /device:TPU:128, one launch (start us, length us, event | category | flops | bytes accessed | tf_op | source)
XLA Modules:
  0.0 105.9 jit_solution(9955974814209421277)
XLA Ops:
  0.7 0.0 copy-start
  0.7 1.7 %copy-done = bf16[3,3,384,384]{3,2,1,0:T(8,128)(2,1)S(1)} copy-done((bf16[3,3,384,384]{3,2,1,0:T(8,128)(2,1)S(1)}, bf16[3,3,384,384]{3,2,1,0:T(8,128)(2,1)}, u32[]{:S(2)}) %copy-start) | copy-done | bytes 2654232
  2.4 0.0 copy-start.1
  2.4 1.1 %copy-done.1 = bf16[32,32,384]{2,1,0:T(8,128)(2,1)S(1)} copy-done((bf16[32,32,384]{2,1,0:T(8,128)(2,1)S(1)}, bf16[32,32,384]{2,1,0:T(8,128)(2,1)}, u32[]{:S(2)}) %copy-start.1) | copy-done | bytes 786456
  3.5 0.0 copy-start.2
  3.5 1.0 copy-done.2
  4.6 100.4 %dilated_block.1 = bf16[64,16,384]{2,1,0:T(8,128)(2,1)S(1)} custom-call(s32[1]{0:T(128)S(6)} %copy.6.lead, bf16[64,16,384]{2,1,0:T(8,128)(2,1)S(1)} %bitcast.3, bf16[3,3,384,384]{3,2,1,0:T(8,128)(2,1)S(1)} %copy-done, bf16[360,2,384]{2,1,0:T(2,128)(2,1)S(1)} %copy-done.2), custom_call_target="tpu_custom_call" | custom-call | flops 2717908992 | bytes 5000000 | tf_op jit(solution)/shard_map/dilated_block/pallas_call | solution.py:239
  105.0 0.9 copy.7
Async XLA Ops:
  0.7 1.8 %copy-start = (bf16[3,3,384,384]{3,2,1,0:T(8,128)(2,1)S(1)}, bf16[3,3,384,384]{3,2,1,0:T(8,128)(2,1)}, u32[]{:S(2)}) copy-start(bf16[3,3,384,384]{3,2,1,0:T(8,128)(2,1)} %w_hbm.1) | copy-start | bytes 7962628
  2.4 1.1 %copy-start.1 = (bf16[32,32,384]{2,1,0:T(8,128)(2,1)S(1)}, bf16[32,32,384]{2,1,0:T(8,128)(2,1)}, u32[]{:S(2)}) copy-start(bf16[32,32,384]{2,1,0:T(8,128)(2,1)} %param.4) | copy-start | bytes 2359300
  3.5 1.1 copy-start.2

commit v2 on v0

v2 whole, which is shorter than its diff:
```python
import functools

import jax
import jax.numpy as jnp
from jax import lax
from jax.experimental import pallas as pl
from jax.experimental.pallas import tpu as pltpu
from jax.sharding import PartitionSpec as P

DILATION_RATE = 128
CHUNKS = 8
RAW = 3
LAG = 2
SETTLE = 2
CELLS = 16
VMEM_LIMIT = 40 * 1024 * 1024
MESH = pl.DeviceIdType.MESH


def kernel(dims, lead, enc_hbm, w_hbm, film_hbm, out, enc, w, film, mid, left, right, hop, raw, acc, done,
           load_sem, own_sem, in_send, in_recv, col_send, col_recv, raw_own, raw_send, raw_recv,
           out_send, out_recv):
    n_rows, n_cols, row_step, hops = dims
    per = enc.shape[1]
    take = per // CHUNKS
    chans = enc.shape[-1]
    cells = n_rows * take * CELLS
    row, col = lax.axis_index("rows"), lax.axis_index("cols")
    me, lane = row // row_step, row % row_step
    last_col = n_cols * hops - 1
    sides = (left, right)
    inside = pl.ds(1, n_rows)

    def peer(step):
        other = lax.rem(me + step, n_rows)
        return other, (other * row_step + lane, col)

    def source(step):
        return lax.rem(me + n_rows - step, n_rows)

    def each(first, last, act):
        def body(step, carry):
            act(step)
            return carry
        lax.fori_loop(first, last, body, 0)

    def holds(stage, way):
        if way == 0:
            return jnp.logical_and(col >= stage, col - stage <= last_col - hops)
        return jnp.logical_and(col + stage >= hops, col + stage <= last_col)

    loads = [
        pltpu.make_async_copy(enc_hbm, enc, load_sem.at[0]),
        pltpu.make_async_copy(w_hbm, w, load_sem.at[1]),
        pltpu.make_async_copy(film_hbm, film, load_sem.at[2]),
    ]
    for load in loads:
        load.start()

    barrier = pltpu.get_barrier_semaphore()
    below, above = col > 0, col < last_col

    @pl.when(below)
    def _():
        pl.semaphore_signal(barrier, inc=1, device_id=(row, col - 1), device_id_type=MESH)

    @pl.when(above)
    def _():
        pl.semaphore_signal(barrier, inc=1, device_id=(row, col + 1), device_id_type=MESH)

    each(1, n_rows, lambda step: pl.semaphore_signal(
        barrier, inc=1, device_id=peer(step)[1], device_id_type=MESH))

    for buffer in (mid, left, right):
        zero = jnp.zeros(buffer.shape[:1] + buffer.shape[2:], buffer.dtype)
        buffer[:, 0] = zero
        buffer[:, n_rows + 1] = zero

    for way in range(2):
        @pl.when(jnp.logical_not(holds(hops, way)))
        def _():
            sides[way][...] = jnp.zeros_like(sides[way])

    loads[0].wait()
    greeted = n_rows - 1 + below.astype(jnp.int32) + above.astype(jnp.int32)
    pl.semaphore_wait(barrier, greeted)

    def own_copy(part):
        return pltpu.make_async_copy(
            enc.at[me, pl.ds(part * take, take)], mid.at[part, me + 1], own_sem.at[part])

    def in_copy(part, step):
        other, device = peer(step)
        return pltpu.make_async_remote_copy(
            src_ref=enc.at[other, pl.ds(part * take, take)],
            dst_ref=mid.at[part, me + 1],
            send_sem=in_send.at[part],
            recv_sem=in_recv.at[part],
            device_id=device, device_id_type=MESH)

    others = pl.ds(0, n_rows - 1)

    def in_all(part):
        return pltpu.make_async_remote_copy(
            src_ref=mid.at[part, others], dst_ref=mid.at[part, others],
            send_sem=in_send.at[part], recv_sem=in_recv.at[part],
            device_id=peer(1)[1], device_id_type=MESH)

    def spread(part):
        own_copy(part).start()
        each(1, n_rows, lambda step: in_copy(part, step).start())

    def col_copy(part, stage, way, first=False, final=False):
        if stage > 0:
            src = hop.at[way, stage - 1, part]
        elif first:
            src = enc.at[:, pl.ds(part * take, take)]
        else:
            src = mid.at[part, inside]
        if stage < hops - 1:
            dst = hop.at[way, stage, part]
        elif final:
            dst = raw.at[way, part]
        else:
            dst = sides[way].at[part, inside]
        return pltpu.make_async_remote_copy(
            src_ref=src, dst_ref=dst,
            send_sem=col_send.at[way, stage, part],
            recv_sem=col_recv.at[way, stage, part],
            device_id=(row, col + (1, -1)[way]), device_id_type=MESH)

    def depart(part, first):
        for way in range(2):
            @pl.when(holds(0, way))
            def _():
                col_copy(part, 0, way, first=first).start()

    def relay(part, stage):
        for way in range(2):
            @pl.when(holds(stage, way))
            def _():
                col_copy(part, stage - 1, way).wait_recv()
                if stage < hops - 1:
                    col_copy(part, stage, way).start()
                else:
                    @pl.when(part < RAW)
                    def _():
                        col_copy(part, stage, way, final=True).start()

                    @pl.when(part >= RAW)
                    def _():
                        col_copy(part, stage, way).start()

    def land(part):
        for way in range(2):
            @pl.when(holds(hops, way))
            def _():
                col_copy(part, hops - 1, way).wait_recv()

    def raw_own_copy(part, way):
        return pltpu.make_async_copy(
            raw.at[way, part, me], sides[way].at[part, me + 1], raw_own.at[way, part])

    def raw_copy(part, way, step):
        other, device = peer(step)
        return pltpu.make_async_remote_copy(
            src_ref=raw.at[way, part, other],
            dst_ref=sides[way].at[part, me + 1],
            send_sem=raw_send.at[way, part],
            recv_sem=raw_recv.at[way, part],
            device_id=device, device_id_type=MESH)

    def raw_all(part, way):
        return pltpu.make_async_remote_copy(
            src_ref=raw.at[way, part, others], dst_ref=sides[way].at[part, others],
            send_sem=raw_send.at[way, part], recv_sem=raw_recv.at[way, part],
            device_id=peer(1)[1], device_id_type=MESH)

    def raw_spread(part):
        for way in range(2):
            @pl.when(holds(hops, way))
            def _():
                raw_own_copy(part, way).start()
                each(1, n_rows, lambda step: raw_copy(part, way, step).start())

    def raw_land(part):
        for way in range(2):
            @pl.when(holds(hops, way))
            def _():
                raw_own_copy(part, way).wait()
                raw_all(part, way).wait_recv()

    def out_copy(part, step):
        other, device = peer(step)
        return pltpu.make_async_remote_copy(
            src_ref=done.at[part, other],
            dst_ref=out.at[me, pl.ds(part * take, take)],
            send_sem=out_send.at[part],
            recv_sem=out_recv.at[part],
            device_id=device, device_id_type=MESH)

    def out_all(part):
        return pltpu.make_async_remote_copy(
            src_ref=done.at[part, others], dst_ref=done.at[part, others],
            send_sem=out_send.at[part], recv_sem=out_recv.at[part],
            device_id=peer(1)[1], device_id_type=MESH)

    def out_own(part):
        return pltpu.make_async_copy(
            done.at[part, me], out.at[me, pl.ds(part * take, take)], own_sem.at[CHUNKS + part])

    def taps(part, kx, buffer):
        total = None
        for ky in range(3):
            block = jnp.maximum(buffer[part, pl.ds(ky, n_rows)], 0).reshape(cells, chans)
            term = jnp.dot(block, w[ky, kx], preferred_element_type=jnp.float32)
            total = term if total is None else total + term
        return total

    def update(part):
        picked = film[lead[0]].astype(jnp.float32)
        gamma, beta = picked[0:1], picked[1:2]
        total = acc[part] + taps(part, 0, left) + taps(part, 2, right)
        here = mid[part, inside].reshape(cells, chans).astype(jnp.float32)
        updated = here + total * (1.0 + gamma) + beta
        done[part] = updated.astype(jnp.bfloat16).reshape(done.shape[1:])
        out_own(part).start()
        each(1, n_rows, lambda step: out_copy(part, step).start())

    def both(a, b):
        return jnp.logical_and(a, b)

    for part in range(RAW):
        depart(part, True)
    spread(RAW)
    spread(RAW + 1)
    for load in loads[1:]:
        load.wait()
    crossing = hops * LAG

    def round_(turn, carry):
        shared = both(turn >= RAW, turn < CHUNKS + RAW)
        arriving = lax.rem(turn, CHUNKS)

        @pl.when(shared)
        def _():
            own_copy(arriving).wait()
            in_all(arriving).wait_recv()

        @pl.when(both(shared, turn < CHUNKS))
        def _():
            depart(arriving, False)

        for stage in range(1, hops):
            part = turn - stage * LAG

            @pl.when(both(part >= 0, part < CHUNKS))
            def _():
                relay(part, stage)

        @pl.when(both(shared, turn + 2 < CHUNKS + RAW))
        def _():
            spread(lax.rem(turn + 2, CHUNKS))

        @pl.when(shared)
        def _():
            acc[arriving] = taps(arriving, 1, mid)
            in_all(arriving).wait_send()

        for stage in range(hops):
            sent = turn - stage * LAG - LAG

            @pl.when(both(sent >= 0, sent < CHUNKS))
            def _():
                for way in range(2):
                    @pl.when(holds(stage, way))
                    def _():
                        col_copy(sent, stage, way).wait_send()

        part = turn - crossing

        @pl.when(both(part >= 0, part < CHUNKS))
        def _():
            land(part)

        @pl.when(both(part >= 0, part < RAW))
        def _():
            raw_spread(part)

        def finished(late, carry):
            ready = part - late * SETTLE

            @pl.when(both(late == 1, both(ready >= 0, ready < RAW)))
            def _():
                raw_land(ready)
                for way in range(2):
                    @pl.when(holds(hops, way))
                    def _():
                        raw_all(ready, way).wait_send()

            @pl.when(both(ready >= RAW * (1 - late), ready < jnp.where(late == 1, RAW, CHUNKS)))
            def _():
                update(ready)

            return carry

        lax.fori_loop(0, 2, finished, 0)
        return carry

    lax.fori_loop(0, CHUNKS + crossing, round_, 0)

    def finish(part):
        out_own(part).wait()
        out_all(part).wait_send()
        out_all(part).wait_recv()

    each(0, CHUNKS, finish)


def local(encoded, conv_weight, film_table, lead):
    height, width, chans = encoded.shape
    row_step, hops = DILATION_RATE // height, DILATION_RATE // width
    n_rows = lax.axis_size("rows") // row_step
    n_cols = lax.axis_size("cols") // hops
    per = height * width // CELLS // n_rows
    take = per // CHUNKS
    piece = (take, CELLS, chans)
    bf16, dma = jnp.bfloat16, pltpu.SemaphoreType.DMA
    hbm = pl.BlockSpec(memory_space=pltpu.HBM)
    operands = (encoded.reshape(n_rows, per, CELLS, chans), conv_weight, film_table)
    updated = pl.pallas_call(
        functools.partial(kernel, (n_rows, n_cols, row_step, hops)),
        out_shape=pltpu.VMEM((n_rows, per, CELLS, chans), bf16),
        in_specs=[pl.BlockSpec(memory_space=pltpu.SMEM)] + [hbm] * 3,
        out_specs=pl.BlockSpec(memory_space=pltpu.VMEM),
        scratch_shapes=[
            pltpu.VMEM((n_rows, per, CELLS, chans), bf16),
            pltpu.VMEM(conv_weight.shape, bf16),
            pltpu.VMEM(film_table.shape, bf16),
            pltpu.VMEM((CHUNKS, n_rows + 2) + piece, bf16),
            pltpu.VMEM((CHUNKS, n_rows + 2) + piece, bf16),
            pltpu.VMEM((CHUNKS, n_rows + 2) + piece, bf16),
            pltpu.VMEM((2, hops - 1, CHUNKS, n_rows) + piece, bf16),
            pltpu.VMEM((2, RAW, n_rows) + piece, bf16),
            pltpu.VMEM((CHUNKS, n_rows * take * CELLS, chans), jnp.float32),
            pltpu.VMEM((CHUNKS, n_rows) + piece, bf16),
            dma((3,)),
            dma((2 * CHUNKS,)),
            dma((CHUNKS,)),
            dma((CHUNKS,)),
            dma((2, hops, CHUNKS)),
            dma((2, hops, CHUNKS)),
            dma((2, RAW)),
            dma((2, RAW)),
            dma((2, RAW)),
            dma((CHUNKS,)),
            dma((CHUNKS,)),
        ],
        compiler_params=pltpu.CompilerParams(
            collective_id=0, has_side_effects=True, vmem_limit_bytes=VMEM_LIMIT),
        cost_estimate=pl.CostEstimate(
            flops=2 * 9 * height * width * chans * chans, bytes_accessed=5_000_000, transcendentals=0),
        name="dilated_block",
    )(lead, *(pltpu.with_memory_space_constraint(a, pltpu.HBM) for a in operands))
    return updated.reshape(encoded.shape)


def solution(mesh):
    placed = (P("rows", "cols", None), P(), P(), P())
    return jax.shard_map(
        local, mesh=mesh, in_specs=placed, out_specs=P("rows", "cols", None), check_vma=False
    )
```

time: 265 us -> 85 us (0.32)
  the two profiles are of different devices: /device:TPU:24 before, /device:TPU:192 now
where the time goes in v2:
time: 85 us; the launch traced here: 84.9 us
  Pallas kernels  83.4 us (98%)
  local copies, waits for them, and re-layouts  0.88 us (1%)
    pallas_call x1, Pallas kernels, local(): pl.pallas_call(functools.partial(kernel, (n_rows, n_cols, row_step, hops)...  83.4 us

profile of v2, /device:TPU:192, one launch (start us, length us, event | category | flops | bytes accessed | tf_op | source)
XLA Modules:
  0.0 84.9 jit_solution(13822990057996480595)
XLA Ops:
  0.7 83.4 %dilated_block.1 = bf16[8,8,16,384]{3,2,1,0:T(8,128)(2,1)S(1)} custom-call(s32[1]{0:T(128)S(6)} %copy.7.lead, bf16[8,8,16,384]{3,2,1,0:T(8,128)(2,1)} %bitcast.3, bf16[3,3,384,384]{3,2,1,0:T(8,128)(2,1)} %w_hbm.1, bf16[360,2,384]{2,1,0:T(2,128)(2,1)} %film_hbm.1), custom_call_target="tpu_custom_call" | custom-call | flops 2717908992 | bytes 5000000 | tf_op jit(solution)/shard_map/dilated_block/pallas_call | solution.py:331
  84.0 0.9 %copy.6 = bf16[32,32,384]{2,1,0:T(8,128)(2,1)} copy(bf16[32,32,384]{2,1,0:T(8,128)(2,1)S(1)} %bitcast.2) | data formatting | bytes 1572864

commit v3 on v0

v3 whole, which is shorter than its diff:
```python
import functools

import jax
import jax.numpy as jnp
from jax import lax
from jax.experimental import pallas as pl
from jax.experimental.pallas import tpu as pltpu
from jax.sharding import PartitionSpec as P

DILATION_RATE = 128
CHUNKS = 8
FIRST = 3
LAG = 2
SETTLE = 3
VMEM_LIMIT = 40 * 1024 * 1024
MESH = pl.DeviceIdType.MESH


def kernel(dims, lead, enc_hbm, w_hbm, film_hbm, out, enc, w, film, sides, hop, rows, sums, acc,
           load_sem, col_send, col_recv, row_send, row_recv):
    row_step, hops, last_row, last_col = dims
    row, col = lax.axis_index("rows"), lax.axis_index("cols")

    def both(a, b):
        return jnp.logical_and(a, b)

    def holds(stage, way):
        if way == 0:
            return both(col >= stage, col - stage <= last_col - hops)
        return both(col + stage >= hops, col + stage <= last_col)

    gives = (row <= last_row - row_step, row >= row_step)
    takes = (row >= row_step, row <= last_row - row_step)

    def row_device(way):
        return (row + (row_step, -row_step)[way], col)

    def col_device(way):
        return (row, col + (1, -1)[way])

    loads = [
        pltpu.make_async_copy(enc_hbm, enc, load_sem.at[0]),
        pltpu.make_async_copy(w_hbm, w, load_sem.at[1]),
        pltpu.make_async_copy(film_hbm, film, load_sem.at[2]),
    ]
    for load in loads:
        load.start()

    barrier = pltpu.get_barrier_semaphore()
    greeted = jnp.int32(0)
    for near, device in (
        (col < last_col, col_device(0)), (col > 0, col_device(1)),
        (gives[0], row_device(0)), (gives[1], row_device(1)),
    ):
        @pl.when(near)
        def _():
            pl.semaphore_signal(barrier, inc=1, device_id=device, device_id_type=MESH)

        greeted += near.astype(jnp.int32)

    for way in range(2):
        @pl.when(jnp.logical_not(holds(hops, way)))
        def _():
            sides[way] = jnp.zeros(sides.shape[1:], sides.dtype)

        @pl.when(jnp.logical_not(takes[way]))
        def _():
            rows[way] = jnp.zeros(rows.shape[1:], rows.dtype)

    loads[0].wait()
    pl.semaphore_wait(barrier, greeted)

    def col_copy(part, stage, way, first=False):
        if stage > 0:
            src = hop.at[way, stage - 1, part]
        else:
            src = enc.at[part] if first else sums.at[way, part]
        dst = hop.at[way, stage, part] if stage < hops - 1 else sides.at[way, part]
        return pltpu.make_async_remote_copy(
            src_ref=src, dst_ref=dst,
            send_sem=col_send.at[way, stage, part],
            recv_sem=col_recv.at[way, stage, part],
            device_id=col_device(way), device_id_type=MESH)

    def row_copy(part, way, first=False):
        return pltpu.make_async_remote_copy(
            src_ref=sums.at[way, part] if first else enc.at[part],
            dst_ref=rows.at[way, part],
            send_sem=row_send.at[way, part],
            recv_sem=row_recv.at[way, part],
            device_id=row_device(way), device_id_type=MESH)

    def depart(part, first):
        for way in range(2):
            @pl.when(holds(0, way))
            def _():
                col_copy(part, 0, way, first).start()

    def relay(part, stage):
        for way in range(2):
            @pl.when(holds(stage, way))
            def _():
                col_copy(part, stage - 1, way).wait_recv()
                col_copy(part, stage, way).start()

    def land(part):
        for way in range(2):
            @pl.when(holds(hops, way))
            def _():
                col_copy(part, hops - 1, way).wait_recv()

    def send_rows(part, first):
        for way in range(2):
            @pl.when(gives[way])
            def _():
                row_copy(part, way, first).start()

    def rows_arrived(part):
        for way in range(2):
            @pl.when(takes[way])
            def _():
                row_copy(part, way).wait_recv()

    def rows_sent(part):
        for way in range(2):
            @pl.when(gives[way])
            def _():
                row_copy(part, way).wait_send()

    def active(ref):
        return jnp.maximum(ref[...], 0)

    def tap(block, ky, kx):
        return jnp.dot(block, w[ky, kx], preferred_element_type=jnp.float32)

    def update(part, ends):
        picked = film[lead[0]].astype(jnp.float32)
        gamma, beta = picked[0:1], picked[1:2]
        conv = acc[part, 1] + ends[0, part].astype(jnp.float32) + ends[1, part].astype(jnp.float32)
        out[part] = (enc[part].astype(jnp.float32) + conv * (1.0 + gamma) + beta).astype(jnp.bfloat16)

    def begin_first(part):
        block = active(enc.at[part])
        for ky in range(3):
            acc[part, ky] = tap(block, ky, 1)

    def end_first(part):
        left, right = active(sides.at[0, part]), active(sides.at[1, part])
        for way, ky in ((0, 0), (1, 2)):
            total = acc[part, ky] + tap(left, ky, 0) + tap(right, ky, 2)
            sums[way, part] = total.astype(jnp.bfloat16)
        send_rows(part, True)
        acc[part, 1] += tap(left, 1, 0) + tap(right, 1, 2)

    def prepare(part):
        rows_arrived(part)
        blocks = (active(rows.at[0, part]), active(enc.at[part]), active(rows.at[1, part]))

        def across(kx):
            return tap(blocks[0], 0, kx) + tap(blocks[1], 1, kx) + tap(blocks[2], 2, kx)

        sums[0, part] = across(0).astype(jnp.bfloat16)
        sums[1, part] = across(2).astype(jnp.bfloat16)
        acc[part, 1] = across(1)
        rows_sent(part)

    depart(0, True)
    send_rows(FIRST, False)
    send_rows(FIRST + 1, False)
    for load in loads[1:]:
        load.wait()
    crossing = hops * LAG

    def round_(turn, carry):
        @pl.when(both(turn > 0, turn < FIRST))
        def _():
            depart(turn, True)

        @pl.when(both(turn >= FIRST, turn < CHUNKS))
        def _():
            depart(turn, False)

        for stage in range(1, hops):
            part = turn - stage * LAG

            @pl.when(both(part >= 0, part < CHUNKS))
            def _():
                relay(part, stage)

        @pl.when(both(turn > 0, turn + FIRST + 1 < CHUNKS))
        def _():
            send_rows(turn + FIRST + 1, False)

        @pl.when(turn < FIRST)
        def _():
            begin_first(turn)

        @pl.when(both(turn + 1 >= FIRST, turn + 1 < CHUNKS))
        def _():
            prepare(turn + 1)

        for stage in range(hops):
            sent = turn - stage * LAG - LAG

            @pl.when(both(sent >= 0, sent < CHUNKS))
            def _():
                for way in range(2):
                    @pl.when(holds(stage, way))
                    def _():
                        col_copy(sent, stage, way).wait_send()

        part = turn - crossing

        @pl.when(both(part >= 0, part < CHUNKS))
        def _():
            land(part)

        @pl.when(both(part >= 0, part < FIRST))
        def _():
            end_first(part)

        @pl.when(both(part >= FIRST, part < CHUNKS))
        def _():
            update(part, sides)

        settled = part - SETTLE

        @pl.when(both(settled >= 0, settled < FIRST))
        def _():
            rows_arrived(settled)
            update(settled, rows)
            rows_sent(settled)

        return carry

    lax.fori_loop(0, max(CHUNKS, FIRST + SETTLE) + crossing, round_, 0)


def local(encoded, conv_weight, film_table, lead):
    height, width, chans = encoded.shape
    row_step, hops = DILATION_RATE // height, DILATION_RATE // width
    last_row, last_col = lax.axis_size("rows") - 1, lax.axis_size("cols") - 1
    piece = (height * width // CHUNKS, chans)
    bf16, dma = jnp.bfloat16, pltpu.SemaphoreType.DMA
    hbm = pl.BlockSpec(memory_space=pltpu.HBM)
    operands = (encoded.reshape((CHUNKS,) + piece), conv_weight, film_table)
    updated = pl.pallas_call(
        functools.partial(kernel, (row_step, hops, last_row, last_col)),
        out_shape=pltpu.VMEM((CHUNKS,) + piece, bf16),
        in_specs=[pl.BlockSpec(memory_space=pltpu.SMEM)] + [hbm] * 3,
        out_specs=pl.BlockSpec(memory_space=pltpu.VMEM),
        scratch_shapes=[
            pltpu.VMEM((CHUNKS,) + piece, bf16),
            pltpu.VMEM(conv_weight.shape, bf16),
            pltpu.VMEM(film_table.shape, bf16),
            pltpu.VMEM((2, CHUNKS) + piece, bf16),
            pltpu.VMEM((2, hops - 1, CHUNKS) + piece, bf16),
            pltpu.VMEM((2, CHUNKS) + piece, bf16),
            pltpu.VMEM((2, CHUNKS) + piece, bf16),
            pltpu.VMEM((CHUNKS, 3) + piece, jnp.float32),
            dma((3,)),
            dma((2, hops, CHUNKS)),
            dma((2, hops, CHUNKS)),
            dma((2, CHUNKS)),
            dma((2, CHUNKS)),
        ],
        compiler_params=pltpu.CompilerParams(
            collective_id=0, has_side_effects=True, vmem_limit_bytes=VMEM_LIMIT),
        cost_estimate=pl.CostEstimate(
            flops=2 * 9 * height * width * chans * chans, bytes_accessed=5_000_000, transcendentals=0),
        name="dilated_block",
    )(lead, *(pltpu.with_memory_space_constraint(a, pltpu.HBM) for a in operands))
    return updated.reshape(encoded.shape)


def solution(mesh):
    placed = (P("rows", "cols", None), P(), P(), P())
    return jax.shard_map(
        local, mesh=mesh, in_specs=placed, out_specs=P("rows", "cols", None), check_vma=False
    )
```

time: 265 us -> 78.1 us (0.29)
  the two profiles are of different devices: /device:TPU:24 before, /device:TPU:248 now
where the time goes in v3:
time: 78.1 us; the launch traced here: 77.9 us
  Pallas kernels  76.4 us (98%)
  local copies, waits for them, and re-layouts  0.88 us (1%)
    pallas_call x1, Pallas kernels, local(): pl.pallas_call(functools.partial(kernel, (row_step, hops, last_row, last_...  76.4 us

profile of v3, /device:TPU:248, one launch (start us, length us, event | category | flops | bytes accessed | tf_op | source)
XLA Modules:
  0.0 77.9 jit_solution(2627601449418572232)
XLA Ops:
  0.7 76.4 %dilated_block.1 = bf16[8,128,384]{2,1,0:T(8,128)(2,1)S(1)} custom-call(s32[1]{0:T(128)S(6)} %copy.7.lead, bf16[8,128,384]{2,1,0:T(8,128)(2,1)} %bitcast.3, bf16[3,3,384,384]{3,2,1,0:T(8,128)(2,1)} %w_hbm.1, bf16[360,2,384]{2,1,0:T(2,128)(2,1)} %film_hbm.1), custom_call_target="tpu_custom_call" | custom-call | flops 2717908992 | bytes 5000000 | tf_op jit(solution)/shard_map/dilated_block/pallas_call | solution.py:247
  77.1 0.9 %copy.6 = bf16[32,32,384]{2,1,0:T(8,128)(2,1)} copy(bf16[32,32,384]{2,1,0:T(8,128)(2,1)S(1)} %bitcast.2) | data formatting | bytes 1572864

commit v4 on v3

--- a/solution.py
+++ b/solution.py
@@ -8,10 +8,11 @@
 from jax.sharding import PartitionSpec as P
 
 DILATION_RATE = 128
-CHUNKS = 8
-FIRST = 3
-LAG = 2
-SETTLE = 3
+CHUNKS = 4
+FIRST = 2
+ROUNDS = (0, 1, 2, 3, 4)
+KEEP = 1
+SETTLE = 1
 VMEM_LIMIT = 40 * 1024 * 1024
 MESH = pl.DeviceIdType.MESH
 
@@ -37,6 +38,18 @@
 
     def col_device(way):
         return (row, col + (1, -1)[way])
+
+    barrier = pltpu.get_barrier_semaphore()
+    greeted = jnp.int32(0)
+    for near, device in (
+        (col < last_col, col_device(0)), (col > 0, col_device(1)),
+        (gives[0], row_device(0)), (gives[1], row_device(1)),
+    ):
+        @pl.when(near)
+        def _():
+            pl.semaphore_signal(barrier, inc=1, device_id=device, device_id_type=MESH)
+
+        greeted += near.astype(jnp.int32)
 
     loads = [
         pltpu.make_async_copy(enc_hbm, enc, load_sem.at[0]),
@@ -45,27 +58,6 @@
     ]
     for load in loads:
         load.start()
-
-    barrier = pltpu.get_barrier_semaphore()
-    greeted = jnp.int32(0)
-    for near, device in (
-        (col < last_col, col_device(0)), (col > 0, col_device(1)),
-        (gives[0], row_device(0)), (gives[1], row_device(1)),
-    ):
-        @pl.when(near)
-        def _():
-            pl.semaphore_signal(barrier, inc=1, device_id=device, device_id_type=MESH)
-
-        greeted += near.astype(jnp.int32)
-
-    for way in range(2):
-        @pl.when(jnp.logical_not(holds(hops, way)))
-        def _():
-            sides[way] = jnp.zeros(sides.shape[1:], sides.dtype)
-
-        @pl.when(jnp.logical_not(takes[way]))
-        def _():
-            rows[way] = jnp.zeros(rows.shape[1:], rows.dtype)
 
     loads[0].wait()
     pl.semaphore_wait(barrier, greeted)
@@ -133,11 +125,15 @@
     def tap(block, ky, kx):
         return jnp.dot(block, w[ky, kx], preferred_element_type=jnp.float32)
 
+    def film_row(which):
+        return film[lead[0]].astype(jnp.float32)[which:which + 1]
+
+    def base(part, conv):
+        acc[part, 1] = enc[part].astype(jnp.float32) + conv * (1.0 + film_row(0)) + film_row(1)
+
     def update(part, ends):
-        picked = film[lead[0]].astype(jnp.float32)
-        gamma, beta = picked[0:1], picked[1:2]
-        conv = acc[part, 1] + ends[0, part].astype(jnp.float32) + ends[1, part].astype(jnp.float32)
-        out[part] = (enc[part].astype(jnp.float32) + conv * (1.0 + gamma) + beta).astype(jnp.bfloat16)
+        late = ends[0, part].astype(jnp.float32) + ends[1, part].astype(jnp.float32)
+        out[part] = (acc[part, 1] + late * (1.0 + film_row(0))).astype(jnp.bfloat16)
 
     def begin_first(part):
         block = active(enc.at[part])
@@ -150,7 +146,7 @@
             total = acc[part, ky] + tap(left, ky, 0) + tap(right, ky, 2)
             sums[way, part] = total.astype(jnp.bfloat16)
         send_rows(part, True)
-        acc[part, 1] += tap(left, 1, 0) + tap(right, 1, 2)
+        base(part, acc[part, 1] + tap(left, 1, 0) + tap(right, 1, 2))
 
     def prepare(part):
         rows_arrived(part)
@@ -161,15 +157,24 @@
 
         sums[0, part] = across(0).astype(jnp.bfloat16)
         sums[1, part] = across(2).astype(jnp.bfloat16)
-        acc[part, 1] = across(1)
+        base(part, across(1))
         rows_sent(part)
 
     depart(0, True)
     send_rows(FIRST, False)
-    send_rows(FIRST + 1, False)
+
+    for way in range(2):
+        @pl.when(jnp.logical_not(holds(hops, way)))
+        def _():
+            sides[way] = jnp.zeros(sides.shape[1:], sides.dtype)
+
+        @pl.when(jnp.logical_not(takes[way]))
+        def _():
+            rows[way] = jnp.zeros(rows.shape[1:], rows.dtype)
+
     for load in loads[1:]:
         load.wait()
-    crossing = hops * LAG
+    crossing = ROUNDS[hops]
 
     def round_(turn, carry):
         @pl.when(both(turn > 0, turn < FIRST))
@@ -181,13 +186,13 @@
             depart(turn, False)
 
         for stage in range(1, hops):
-            part = turn - stage * LAG
+            part = turn - ROUNDS[stage]
 
             @pl.when(both(part >= 0, part < CHUNKS))
             def _():
                 relay(part, stage)
 
-        @pl.when(both(turn > 0, turn + FIRST + 1 < CHUNKS))
+        @pl.when(turn + FIRST + 1 < CHUNKS)
         def _():
             send_rows(turn + FIRST + 1, False)
 
@@ -200,7 +205,7 @@
             prepare(turn + 1)
 
         for stage in range(hops):
-            sent = turn - stage * LAG - LAG
+            sent = turn - ROUNDS[stage] - KEEP
 
             @pl.when(both(sent >= 0, sent < CHUNKS))
             def _():

time: 78.1 us -> 77.4 us (level)
  no operation moved by 1% of the time
where the time goes in v4:
time: 77.4 us; the launch traced here: 77.2 us
  Pallas kernels  75.7 us (98%)
  local copies, waits for them, and re-layouts  0.88 us (1%)
    pallas_call x1, Pallas kernels, local(): pl.pallas_call(functools.partial(kernel, (row_step, hops, last_row, last_...  75.7 us

profile of v4, /device:TPU:248, one launch (start us, length us, event | category | flops | bytes accessed | tf_op | source)
XLA Modules:
  0.0 77.2 jit_solution(3211863596724899844)
XLA Ops:
  0.7 75.7 %dilated_block.1 = bf16[4,256,384]{2,1,0:T(8,128)(2,1)S(1)} custom-call(s32[1]{0:T(128)S(6)} %copy.7.lead, bf16[4,256,384]{2,1,0:T(8,128)(2,1)} %bitcast.3, bf16[3,3,384,384]{3,2,1,0:T(8,128)(2,1)} %w_hbm.1, bf16[360,2,384]{2,1,0:T(2,128)(2,1)} %film_hbm.1), custom_call_target="tpu_custom_call" | custom-call | flops 2717908992 | bytes 5000000 | tf_op jit(solution)/shard_map/dilated_block/pallas_call | solution.py:252
  76.4 0.9 %copy.6 = bf16[32,32,384]{2,1,0:T(8,128)(2,1)} copy(bf16[32,32,384]{2,1,0:T(8,128)(2,1)S(1)} %bitcast.2) | data formatting | bytes 1572864

commit v5 on v4

--- a/solution.py
+++ b/solution.py
@@ -18,7 +18,7 @@
 
 
 def kernel(dims, lead, enc_hbm, w_hbm, film_hbm, out, enc, w, film, sides, hop, rows, sums, acc,
-           load_sem, col_send, col_recv, row_send, row_recv):
+           load_sem, col_send, col_recv, row_send, row_recv, vouch_sem, open_sem):
     row_step, hops, last_row, last_col = dims
     row, col = lax.axis_index("rows"), lax.axis_index("cols")
 
@@ -39,11 +39,14 @@
     def col_device(way):
         return (row, col + (1, -1)[way])
 
+    place = lax.rem(col, hops)
+    broker = both(place > 0, place < hops - 1)
+    client = (row, col + jnp.where(place < hops // 2, -1, 1))
     barrier = pltpu.get_barrier_semaphore()
     greeted = jnp.int32(0)
     for near, device in (
         (col < last_col, col_device(0)), (col > 0, col_device(1)),
-        (gives[0], row_device(0)), (gives[1], row_device(1)),
+        (both(broker, gives[0]), row_device(0)), (both(broker, gives[1]), row_device(1)),
     ):
         @pl.when(near)
         def _():
@@ -95,6 +98,12 @@
                 col_copy(part, stage - 1, way).wait_recv()
                 col_copy(part, stage, way).start()
 
+    def left_behind(part, stage):
+        for way in range(2):
+            @pl.when(holds(stage, way))
+            def _():
+                col_copy(part, stage, way).wait_send()
+
     def land(part):
         for way in range(2):
             @pl.when(holds(hops, way))
@@ -160,8 +169,8 @@
         base(part, across(1))
         rows_sent(part)
 
-    depart(0, True)
-    send_rows(FIRST, False)
+    for part in range(FIRST):
+        depart(part, True)
 
     for way in range(2):
         @pl.when(jnp.logical_not(holds(hops, way)))
@@ -174,71 +183,61 @@
 
     for load in loads[1:]:
         load.wait()
+    for part in range(FIRST):
+        begin_first(part)
+
+    @pl.when(broker)
+    def _():
+        for way in range(2):
+            @pl.when(gives[way])
+            def _():
+                pl.semaphore_signal(vouch_sem, inc=1, device_id=row_device(way), device_id_type=MESH)
+
+        pl.semaphore_wait(vouch_sem, takes[0].astype(jnp.int32) + takes[1].astype(jnp.int32))
+        pl.semaphore_signal(open_sem, inc=1, device_id=client, device_id_type=MESH)
+
+    @pl.when(jnp.logical_not(broker))
+    def _():
+        pl.semaphore_wait(open_sem, 1)
+
+    send_rows(FIRST, False)
     crossing = ROUNDS[hops]
 
-    def round_(turn, carry):
-        @pl.when(both(turn > 0, turn < FIRST))
-        def _():
-            depart(turn, True)
-
-        @pl.when(both(turn >= FIRST, turn < CHUNKS))
-        def _():
-            depart(turn, False)
-
+    for turn in range(1, max(CHUNKS, FIRST + SETTLE) + crossing):
         for stage in range(1, hops):
             part = turn - ROUNDS[stage]
-
-            @pl.when(both(part >= 0, part < CHUNKS))
-            def _():
+            if 0 <= part < FIRST:
                 relay(part, stage)
 
-        @pl.when(turn + FIRST + 1 < CHUNKS)
-        def _():
-            send_rows(turn + FIRST + 1, False)
-
-        @pl.when(turn < FIRST)
-        def _():
-            begin_first(turn)
-
-        @pl.when(both(turn + 1 >= FIRST, turn + 1 < CHUNKS))
-        def _():
-            prepare(turn + 1)
+        if FIRST <= turn < CHUNKS:
+            prepare(turn)
+            depart(turn, False)
+            if turn + 1 < CHUNKS:
+                send_rows(turn + 1, False)
+
+        for stage in range(1, hops):
+            part = turn - ROUNDS[stage]
+            if FIRST <= part < CHUNKS:
+                relay(part, stage)
 
         for stage in range(hops):
             sent = turn - ROUNDS[stage] - KEEP
-
-            @pl.when(both(sent >= 0, sent < CHUNKS))
-            def _():
-                for way in range(2):
-                    @pl.when(holds(stage, way))
-                    def _():
-                        col_copy(sent, stage, way).wait_send()
+            if 0 <= sent < CHUNKS:
+                left_behind(sent, stage)
 
         part = turn - crossing
-
-        @pl.when(both(part >= 0, part < CHUNKS))
-        def _():
+        if 0 <= part < CHUNKS:
             land(part)
-
-        @pl.when(both(part >= 0, part < FIRST))
-        def _():
-            end_first(part)
-
-        @pl.when(both(part >= FIRST, part < CHUNKS))
-        def _():
-            update(part, sides)
+            if part < FIRST:
+                end_first(part)
+            else:
+                update(part, sides)
 
         settled = part - SETTLE
-
-        @pl.when(both(settled >= 0, settled < FIRST))
-        def _():
+        if 0 <= settled < FIRST:
             rows_arrived(settled)
             update(settled, rows)
             rows_sent(settled)
-
-        return carry
-
-    lax.fori_loop(0, max(CHUNKS, FIRST + SETTLE) + crossing, round_, 0)
 
 
 def local(encoded, conv_weight, film_table, lead):
@@ -268,6 +267,8 @@
             dma((2, hops, CHUNKS)),
             dma((2, CHUNKS)),
             dma((2, CHUNKS)),
+            pltpu.SemaphoreType.REGULAR,
+            pltpu.SemaphoreType.REGULAR,
         ],
         compiler_params=pltpu.CompilerParams(
             collective_id=0, has_side_effects=True, vmem_limit_bytes=VMEM_LIMIT),

time: 77.4 us -> 76.2 us (0.984)
  the two profiles are of different devices: /device:TPU:248 before, /device:TPU:184 now
where the time goes in v5:
time: 76.2 us; the launch traced here: 76 us
  Pallas kernels  74.5 us (98%)
  local copies, waits for them, and re-layouts  0.88 us (1%)
    pallas_call x1, Pallas kernels, local(): pl.pallas_call(functools.partial(kernel, (row_step, hops, last_row, last_...  74.5 us

profile of v5, /device:TPU:184, one launch (start us, length us, event | category | flops | bytes accessed | tf_op | source)
XLA Modules:
  0.0 76.0 jit_solution(16308320379503732093)
XLA Ops:
  0.7 74.5 %dilated_block.1 = bf16[4,256,384]{2,1,0:T(8,128)(2,1)S(1)} custom-call(s32[1]{0:T(128)S(6)} %copy.7.lead, bf16[4,256,384]{2,1,0:T(8,128)(2,1)} %bitcast.3, bf16[3,3,384,384]{3,2,1,0:T(8,128)(2,1)} %w_hbm.1, bf16[360,2,384]{2,1,0:T(2,128)(2,1)} %film_hbm.1), custom_call_target="tpu_custom_call" | custom-call | flops 2717908992 | bytes 5000000 | tf_op jit(solution)/shard_map/dilated_block/pallas_call | solution.py:251
  75.2 0.9 %copy.6 = bf16[32,32,384]{2,1,0:T(8,128)(2,1)} copy(bf16[32,32,384]{2,1,0:T(8,128)(2,1)S(1)} %bitcast.2) | data formatting | bytes 1572864

commit v6 on v5

--- a/solution.py
+++ b/solution.py
@@ -104,8 +104,8 @@
             def _():
                 col_copy(part, stage, way).wait_send()
 
-    def land(part):
-        for way in range(2):
+    def land(part, ways):
+        for way in ways:
             @pl.when(holds(hops, way))
             def _():
                 col_copy(part, hops - 1, way).wait_recv()
@@ -183,9 +183,6 @@
 
     for load in loads[1:]:
         load.wait()
-    for part in range(FIRST):
-        begin_first(part)
-
     @pl.when(broker)
     def _():
         for way in range(2):
@@ -201,6 +198,9 @@
         pl.semaphore_wait(open_sem, 1)
 
     send_rows(FIRST, False)
+    for part in range(FIRST):
+        begin_first(part)
+
     crossing = ROUNDS[hops]
 
     for turn in range(1, max(CHUNKS, FIRST + SETTLE) + crossing):
@@ -227,11 +227,15 @@
 
         part = turn - crossing
         if 0 <= part < CHUNKS:
-            land(part)
             if part < FIRST:
+                land(part, (0, 1))
                 end_first(part)
             else:
-                update(part, sides)
+                land(part, (0,))
+                acc[part, 1] += sides[0, part].astype(jnp.float32) * (1.0 + film_row(0))
+                land(part, (1,))
+                late = sides[1, part].astype(jnp.float32)
+                out[part] = (acc[part, 1] + late * (1.0 + film_row(0))).astype(jnp.bfloat16)
 
         settled = part - SETTLE
         if 0 <= settled < FIRST:

time: 76.2 us -> 76.1 us (level)
  the two profiles are of different devices: /device:TPU:184 before, /device:TPU:152 now
where the time goes in v6:
time: 76.1 us; the launch traced here: 76 us
  Pallas kernels  74.5 us (98%)
  local copies, waits for them, and re-layouts  0.88 us (1%)
    pallas_call x1, Pallas kernels, local(): pl.pallas_call(functools.partial(kernel, (row_step, hops, last_row, last_...  74.5 us

profile of v6, /device:TPU:152, one launch (start us, length us, event | category | flops | bytes accessed | tf_op | source)
XLA Modules:
  0.0 76.0 jit_solution(3827133419046785128)
XLA Ops:
  0.7 74.5 %dilated_block.1 = bf16[4,256,384]{2,1,0:T(8,128)(2,1)S(1)} custom-call(s32[1]{0:T(128)S(6)} %copy.7.lead, bf16[4,256,384]{2,1,0:T(8,128)(2,1)} %bitcast.3, bf16[3,3,384,384]{3,2,1,0:T(8,128)(2,1)} %w_hbm.1, bf16[360,2,384]{2,1,0:T(2,128)(2,1)} %film_hbm.1), custom_call_target="tpu_custom_call" | custom-call | flops 2717908992 | bytes 5000000 | tf_op jit(solution)/shard_map/dilated_block/pallas_call | solution.py:255
  75.1 0.9 %copy.6 = bf16[32,32,384]{2,1,0:T(8,128)(2,1)} copy(bf16[32,32,384]{2,1,0:T(8,128)(2,1)S(1)} %bitcast.2) | data formatting | bytes 1572864
